TPU v7x, 256 devices: a whole 4x4x8 slice. The times are simulated.
256 devices in a mesh: pts: 128 (over y, x, z_hi, core), rhs: 2 (over z_lo).
Axes of the slice: x: 4, y: 4, z: 8 (z_hi: 4, z_lo: 2; z = z_hi * 2 + z_lo), core: 2. Of those that a mesh axis runs over, the one named last changes fastest.
Arguments:
- right_sides: bfloat16 [64, 524288], P('rhs', 'pts'), may hold values from -6 to 6
- morton: int32 [524288], P('pts'), may hold values from 0 to 524287, as said below
- near_leaf: int32 [256], P('pts'), may hold values from 0 to 255, as said below
- points: bfloat16 [64, 524288], P(None, 'pts'), may hold values from -5 to 5
- far_left: bfloat16 [8, 64, 524288], P(None, None, 'pts'), may hold values from -0.25 to 0.25
- far_right: bfloat16 [8, 64, 524288], P(None, None, 'pts'), may hold values from -4 to 4, as said below
Outputs:
- first_product: float32 [64, 524288], P('rhs', 'pts')
- second_product: float32 [64, 524288], P('rhs', 'pts')
Inputs may be any that keep to these rules, and one draw needn't show every extreme that they name: `morton`: each block of 4096 consecutive entries holds the indices of that same block in some order. `near_leaf`: for an even leaf i the entry is i - 1 or i - 2, for an odd leaf i + 1 or i + 2, clipped to the range of leaves. `far_right`: entries of level k are at most 4 / sqrt(2048 * 2^k) in magnitude.
All inputs are finite; a program needn't handle non-finite values.
Results may differ from a plain program's by a relative error of at most 0.0028.
Values may be sent and summed in bfloat16 or wider, within the bound.
A program may use at most 128 MiB of HBM per device.

v0:
```python
import jax
import jax.numpy as jnp
from jax import lax
from jax.experimental import pallas as pl
from jax.experimental.pallas import tpu as pltpu
from jax.sharding import PartitionSpec as P

DIM = 64
LEAF = 2048
RANK = 64
LEVELS = 8
ROWS = 32
HALF = 16
WIDTH = LEVELS * RANK
BLOCK = 2 * LEAF
DEPTH = 128
MESH = pl.DeviceIdType.MESH
F32 = jnp.float32
BF16 = jnp.bfloat16


def dot(a, b):
    return jnp.dot(a, b, preferred_element_type=F32)


def dot_nt(a, b):
    return lax.dot_general(a, b, (((1,), (1,)), ((), ())), preferred_element_type=F32)


def norm_rows(x, first):
    wide = x.astype(F32)
    a = jnp.sum(wide * wide, axis=0, keepdims=True) * (-1.0 / 32.0)
    h1 = a.astype(BF16).astype(F32)
    r1 = a - h1
    h2 = r1.astype(BF16).astype(F32)
    h3 = r1 - h2
    row = lax.broadcasted_iota(jnp.int32, (8, x.shape[1]), 0) - first
    one = jnp.where((row >= 3 - 2 * first) & (row < 6 - 2 * first), 1.0, 0.0)
    return jnp.where(row == 0, h1, jnp.where(row == 1, h2, jnp.where(row == 2, h3, one)))


def kernel(
    near, morton, rs_hbm, pts_hbm, fl_hbm, fr_hbm,
    out1, out2,
    tiles, fl, fr, pts, halo_pts, stage_pts, rs, vals, halo_vals, stage_vals,
    src, tgt, acc, far_sum, sel_out, sel_in,
    coef, p0_in, p1_sum, p1_out, p1_in, p1_out_short, p1_in_short, p2_out, p2_in, sib_low, sib_high, sib,
    local_sem, out_sem, send_sem, recv_sem,
):
    pos = lax.axis_index("pts")
    count = lax.axis_size("pts")
    core = lax.rem(pos, 2)
    mate = pos + 1 - 2 * core
    beyond = lax.rem(pos + count - 1 + 2 * core, count)
    near_slot, far_slot = 1 - core, core
    inner = jnp.logical_and(pos > 0, pos < count - 1)

    def shifted(shift, d):
        digit = lax.rem(pos // shift, 4)
        if d == 0:
            return 0
        if d == 1:
            other = digit + 1 - 2 * lax.rem(digit, 2)
        elif d == 2:
            other = lax.rem(digit + 2, 4)
        else:
            other = 3 - digit
        return (other - digit) * shift

    z_peers = [pos + shifted(2, d) for d in (1, 2, 3)]
    xy_peers = [pos + shifted(8, d % 4) + shifted(32, d // 4) for d in range(1, 16)]

    load_rs = pltpu.make_async_copy(rs_hbm, rs, local_sem.at[0])
    load_pts = [
        pltpu.make_async_copy(pts_hbm.at[:, pl.ds(l * LEAF, LEAF)], pts.at[l], local_sem.at[1 + l]) for l in range(2)
    ]
    load_fr = pltpu.make_async_copy(fr_hbm, fr, local_sem.at[3])
    load_fl = pltpu.make_async_copy(fl_hbm, fl, local_sem.at[4])
    load_rs.start()
    load_pts[0].start()
    load_pts[1].start()
    load_fr.start()
    load_fl.start()

    barrier = pltpu.get_barrier_semaphore()
    everyone = [mate, beyond] + z_peers + xy_peers
    for peer in everyone:
        pl.semaphore_signal(barrier, inc=1, device_id={"pts": peer}, device_id_type=MESH)

    slot = [0]
    sent = []

    def remote(source, target, peer, track=True):
        i = slot[0]
        slot[0] += 1
        copy = pltpu.make_async_remote_copy(
            src_ref=source, dst_ref=target, send_sem=send_sem.at[i], recv_sem=recv_sem.at[i],
            device_id={"pts": peer}, device_id_type=MESH,
        )
        if track:
            sent.append(copy)
        return copy

    class Beyond:
        def __init__(self, source, target):
            self.copy = remote(source, target, beyond, False)
            sent.append(self)

        def start(self):
            pl.when(inner)(self.copy.start)

        def wait_recv(self):
            pl.when(inner)(self.copy.wait_recv)

        def wait_send(self):
            pl.when(inner)(self.copy.wait_send)

    wanted = [near[0] - 2 * pos + 2, near[1] - 2 * pos - 2]
    sel_out[0] = jnp.full((8, 128), jnp.where(core == 0, wanted[1], wanted[0]).astype(F32))
    sel_out[1] = jnp.full((8, 128), jnp.where(core == 0, wanted[0], wanted[1]).astype(F32))

    pl.semaphore_wait(barrier, len(everyone))
    sel_far = Beyond(sel_out.at[1], sel_in.at[1])
    sel_far.start()
    sel_mate = remote(sel_out.at[0], sel_in.at[0], mate)
    sel_mate.start()

    load_rs.wait()
    folded = jnp.concatenate([rs[:, h * 256 : (h + 1) * 256] for h in range(16)], axis=0)

    def permute(l):
        step = 1024
        for j in range(LEAF // step):
            at = l * LEAF + j * step
            index = morton[:, at : at + step] - pos * BLOCK
            low = index & 255
            high = index >> 8
            hot = jnp.where(lax.broadcasted_iota(jnp.int32, (256, step), 0) == low, 1.0, 0.0).astype(BF16)
            picked = dot(folded, hot)
            total = jnp.zeros((ROWS, step), F32)
            for h in range(16):
                total = jnp.where(high == h, picked[h * ROWS : (h + 1) * ROWS], total)
            vals[0, l, :, j * step : (j + 1) * step] = total.astype(BF16)

    permute(0)
    permute(1)
    def stage(source, target, side):
        chosen = sel_in[side, 0:1, 0:1] > 0.5
        target[side] = jnp.where(chosen, source[1].astype(F32), source[0].astype(F32)).astype(BF16)

    def edges(own, landing):
        @pl.when(pos == 0)
        def _():
            landing[1] = own[0]

        @pl.when(pos == count - 1)
        def _():
            landing[1] = own[1]

    lane = lax.broadcasted_iota(jnp.int32, (HALF, 128), 1)

    def halves(first, second):
        return jnp.where(lane < 64, first, second)

    class Exchange:
        def __init__(self, prod):
            self.prod = prod

        def start(self):
            prod = self.prod
            c = [dot_nt(vals[prod, l], fr[:, l * LEAF : (l + 1) * LEAF]) for l in range(2)]
            both = c[0] + c[1]
            for h in range(2):
                coef[prod, h] = both[h * HALF : (h + 1) * HALF]
            self.copies = [remote(coef.at[prod], p0_in.at[prod], mate)]
            self.copies[0].start()
            for l in range(2):
                sib[l, :, 0:128] = c[1 - l][:, 0:128].astype(BF16)

        def arrived(self):
            for copy in self.copies:
                copy.wait_recv()

        def after_core(self):
            prod = self.prod
            self.arrived()
            p1_sum[...] = coef[prod, core, :, 128:] + p0_in[prod, core, :, 128:]
            out, arrivals = ((p1_out, p1_in), (p1_out_short, p1_in_short))[prod]
            out[...] = p1_sum[...].astype(out.dtype)
            self.copies = [remote(out, arrivals.at[d], z_peers[d]) for d in range(3)]
            for copy in self.copies:
                copy.start()
            for l in range(2):
                for h in range(2):
                    rows = pl.ds(h * HALF, HALF)
                    sib[l, rows, 0:128] = halves(
                        sib[l, rows, 0:128].astype(F32), p0_in[prod, h, :, 0:128]
                    ).astype(BF16)

        def after_z(self):
            prod = self.prod
            self.arrived()
            arrivals = (p1_in, p1_in_short)[prod]
            a, b, c = [arrivals[d].astype(F32) for d in range(3)]
            for t in range(2):
                cols = slice(128 + 128 * t, 256 + 128 * t)
                p2_out[prod, t] = (p1_sum[:, cols] + a[:, cols]) + (b[:, cols] + c[:, cols])
            self.copies = [
                remote(p2_out.at[prod, 0 if d < 4 else 1], p2_in.at[prod, d - 1], xy_peers[d - 1]) for d in range(1, 16)
            ]
            for copy in self.copies:
                copy.start()
            sib_low[prod, core] = halves(a[:, 0:128], b[:, 0:128] + c[:, 0:128]).astype(BF16)
            self.low = remote(sib_low.at[prod, core], sib_low.at[prod, core], mate)
            self.low.start()

        def after_xy(self):
            prod = self.prod
            self.arrived()

            def total(lo, hi):
                value = p2_in[prod, lo - 1]
                for d in range(lo + 1, hi):
                    value = value + p2_in[prod, d - 1]
                return value

            sib_high[prod, core, :, 0:128] = halves(total(1, 2), total(2, 4)).astype(BF16)
            sib_high[prod, core, :, 128:256] = halves(total(4, 8), total(8, 16)).astype(BF16)
            self.copies = [remote(sib_high.at[prod, core], sib_high.at[prod, core], mate)]
            self.copies[0].start()

        def finish_low(self):
            self.low.wait_recv()
            for l in range(2):
                for h in range(2):
                    sib[l, pl.ds(h * HALF, HALF), 128:256] = sib_low[self.prod, h]

        def finish_high(self):
            self.arrived()
            for l in range(2):
                for h in range(2):
                    sib[l, pl.ds(h * HALF, HALF), 256:] = sib_high[self.prod, h]

    def far(l, part):
        rows = slice(part * 256, part * 256 + 256)
        return dot(sib[l, :, rows], fl[rows, l * LEAF : (l + 1) * LEAF])

    def prepare_source(x):
        rows = norm_rows(x, 0)
        whole = jnp.concatenate([x.astype(F32), rows, jnp.zeros((DEPTH - DIM - 8, LEAF), F32)], axis=0)
        src[...] = whole.T.astype(BF16)

    def prepare_target(l):
        x = pts[l]
        rows = norm_rows(x, 3)
        whole = jnp.concatenate(
            [x.astype(F32) * (1.0 / 16.0), rows, jnp.zeros((DEPTH - DIM - 8, LEAF), F32)], axis=0
        )
        tgt[l] = whole.astype(BF16)

    def generate(tile, l, values, part):
        at = part * 1024
        for j in range(4):
            cols = pl.ds(j * 512, 512)
            exponent = dot(src[at : at + 1024, :], tgt[l, :, cols])
            made = jnp.exp(exponent).astype(BF16)
            tiles[tile, at : at + 1024, cols] = made
            acc[l, :, cols] += dot(values[:, at : at + 1024], made)

    def apply(tile, l, values, part, first=False):
        cols = pl.ds(part * 1024, 1024)
        value = dot(values[...], tiles[tile, :, cols])
        acc[l, :, cols] = value if first else acc[l, :, cols] + value

    load_pts[0].wait()
    load_pts[1].wait()
    def halo_values(prod):
        return (
            remote(stage_vals.at[prod, 0], halo_vals.at[prod, 0], mate),
            Beyond(stage_vals.at[prod, 1], halo_vals.at[prod, 1]),
        )

    load_fr.wait()
    first = Exchange(0)
    first.start()
    acc[...] = jnp.zeros_like(acc)
    for l in range(2):
        prepare_target(l)
    prepare_source(pts[0])
    sel_far.wait_recv()
    stage(pts, stage_pts, 1)
    stage(vals.at[0], stage_vals.at[0], 1)
    first.after_core()
    pts_far = Beyond(stage_pts.at[1], halo_pts.at[1])
    pts_far.start()
    vals_mate, vals_far = halo_values(0)
    vals_far.start()
    generate(0, 0, vals.at[0, 0], 0)
    sel_mate.wait_recv()
    stage(pts, stage_pts, 0)
    pts_mate = remote(stage_pts.at[0], halo_pts.at[0], mate)
    pts_mate.start()
    stage(vals.at[0], stage_vals.at[0], 0)
    vals_mate.start()
    generate(0, 0, vals.at[0, 0], 1)
    prepare_source(pts[1])
    generate(1, 1, vals.at[0, 1], 0)
    generate(1, 1, vals.at[0, 1], 1)
    pts_mate.wait_recv()
    vals_mate.wait_recv()
    first.after_z()
    prepare_source(halo_pts[0])
    generate(2, near_slot, halo_vals.at[0, 0], 0)
    generate(2, near_slot, halo_vals.at[0, 0], 1)
    pts_far.wait_recv()
    edges(pts, halo_pts)
    vals_far.wait_recv()
    edges(vals.at[0], halo_vals.at[0])
    prepare_source(halo_pts[1])
    generate(3, far_slot, halo_vals.at[0, 1], 0)
    load_fl.wait()
    first.finish_low()
    for l in range(2):
        acc[l] += far(l, 0)
    first.after_xy()
    generate(3, far_slot, halo_vals.at[0, 1], 1)
    first.finish_high()
    for l in range(2):
        whole = acc[l] + far(l, 1)
        far_sum[l] = whole
        vals[1, l] = whole.astype(BF16)
    outs = [
        pltpu.make_async_copy(far_sum.at[l], out1.at[:, pl.ds(l * LEAF, LEAF)], out_sem.at[l]) for l in range(2)
    ]
    for copy in outs:
        copy.start()

    vals_mate, vals_far = halo_values(1)
    stage(vals.at[1], stage_vals.at[1], 1)
    vals_far.start()
    second = Exchange(1)
    second.start()
    stage(vals.at[1], stage_vals.at[1], 0)
    vals_mate.start()
    apply(0, 0, vals.at[1, 0], 0, True)
    second.after_core()
    apply(0, 0, vals.at[1, 0], 1, True)
    for part in range(2):
        apply(1, 1, vals.at[1, 1], part, True)
    vals_mate.wait_recv()
    for part in range(2):
        apply(2, near_slot, halo_vals.at[1, 0], part)
    second.after_z()
    vals_far.wait_recv()
    edges(vals.at[1], halo_vals.at[1])
    for part in range(2):
        apply(3, far_slot, halo_vals.at[1, 1], part)
    second.finish_low()
    for l in range(2):
        acc[l] += far(l, 0)
    second.after_xy()
    second.finish_high()
    for l in range(2):
        acc[l] += far(l, 1)
    more = [pltpu.make_async_copy(acc.at[l], out2.at[:, pl.ds(l * LEAF, LEAF)], out_sem.at[2 + l]) for l in range(2)]
    for copy in more:
        copy.start()
    for copy in sent:
        copy.wait_send()
    for copy in outs + more:
        copy.wait()


COPIES = 2 + 2 + 2 + 2 + 2 * (1 + 3 + 15 + 2)


def copy_out(first, second, out1, out2, held, sem):
    copies = []
    for t, (source, target) in enumerate(((first, out1), (second, out2))):
        for j in range(2):
            rows = pl.ds(j * HALF, HALF)
            here = held.at[t, rows]
            copies.append((
                pltpu.make_async_copy(source.at[rows], here, sem.at[0, 2 * t + j]),
                pltpu.make_async_copy(here, target.at[rows], sem.at[1, 2 * t + j]),
            ))
    for load, _ in copies:
        load.start()
    for load, store in copies:
        load.wait()
        store.start()
    for _, store in copies:
        store.wait()


def body(right_sides, morton, near_leaf, points, far_left, far_right):
    vmem = pltpu.VMEM
    hbm = pl.BlockSpec(memory_space=pl.ANY)
    out = jax.ShapeDtypeStruct((ROWS, BLOCK), F32)
    results = pl.pallas_call(
        kernel,
        out_shape=(out, out),
        in_specs=[
            pl.BlockSpec(memory_space=pltpu.SMEM),
            pl.BlockSpec(memory_space=pltpu.VMEM),
            hbm, hbm, hbm, hbm,
        ],
        out_specs=(hbm, hbm),
        scratch_shapes=[
            vmem((4, LEAF, LEAF), BF16),
            vmem((WIDTH, BLOCK), BF16),
            vmem((WIDTH, BLOCK), BF16),
            vmem((2, DIM, LEAF), BF16),
            vmem((2, DIM, LEAF), BF16),
            vmem((2, DIM, LEAF), BF16),
            vmem((ROWS, BLOCK), BF16),
            vmem((2, 2, ROWS, LEAF), BF16),
            vmem((2, 2, ROWS, LEAF), BF16),
            vmem((2, 2, ROWS, LEAF), BF16),
            vmem((LEAF, DEPTH), BF16),
            vmem((2, DEPTH, LEAF), BF16),
            vmem((2, ROWS, LEAF), F32),
            vmem((2, ROWS, LEAF), F32),
            vmem((2, 8, 128), F32),
            vmem((2, 8, 128), F32),
            vmem((2, 2, HALF, WIDTH), F32),
            vmem((2, 2, HALF, WIDTH), F32),
            vmem((HALF, 384), F32),
            vmem((HALF, 384), F32),
            vmem((3, HALF, 384), F32),
            vmem((HALF, 384), BF16),
            vmem((3, HALF, 384), BF16),
            vmem((2, 2, HALF, 128), F32),
            vmem((2, 15, HALF, 128), F32),
            vmem((2, 2, HALF, 128), BF16),
            vmem((2, 2, HALF, 256), BF16),
            vmem((2, ROWS, WIDTH), BF16),
            pltpu.SemaphoreType.DMA((5,)),
            pltpu.SemaphoreType.DMA((4,)),
            pltpu.SemaphoreType.DMA((COPIES,)),
            pltpu.SemaphoreType.DMA((COPIES,)),
        ],
        compiler_params=pltpu.CompilerParams(
            collective_id=0, has_side_effects=True, vmem_limit_bytes=60 << 20
        ),
    )(
        near_leaf,
        morton.reshape(1, BLOCK),
        right_sides,
        points,
        far_left.reshape(WIDTH, BLOCK),
        far_right.reshape(WIDTH, BLOCK),
    )
    return pl.pallas_call(
        copy_out,
        out_shape=(out, out),
        in_specs=[hbm, hbm],
        out_specs=(hbm, hbm),
        scratch_shapes=[pltpu.VMEM((2, ROWS, BLOCK), F32), pltpu.SemaphoreType.DMA((2, 4))],
    )(*results)


def solution(mesh):
    placed = (
        P("rhs", "pts"),
        P("pts"),
        P("pts"),
        P(None, "pts"),
        P(None, None, "pts"),
        P(None, None, "pts"),
    )
    return jax.shard_map(
        body,
        mesh=mesh,
        in_specs=placed,
        out_specs=(P("rhs", "pts"), P("rhs", "pts")),
        check_vma=False,
    )
```

profile of v0, /device:TPU:1, one launch (start us, length us, event | category | flops | bytes accessed | tf_op | source)
XLA Modules:
  0.0 53.0 jit_solution(14646716957453405582)
XLA Ops:
  0.6 50.2 %shard_map.77 = (f32[32,4096]{1,0:T(8,128)}, f32[32,4096]{1,0:T(8,128)}) custom-call(s32[2]{0:T(128)} %near.1, s32[1,4096]{1,0:T(1,128)} %bitcast.5, bf16[32,4096]{1,0:T(8,128)(2,1)} %rs_hbm.1, bf16[64,4096]{1,0:T(8,128)(2,1)} %pts_hbm.1, bf16[512,4096]{1,0:T(8,128)(2,1)} %bitcast.3, bf16[512,4096]{1,0:T(8,128)(2,1)} %bitcast.4), custom_call_target="tpu_custom_call" | custom-call | tf_op jit(solution)/shard_map/pallas_call | solution.py:400
  50.9 2.0 %shard_map.78 = (f32[32,4096]{1,0:T(8,128)}, f32[32,4096]{1,0:T(8,128)}) custom-call(f32[32,4096]{1,0:T(8,128)} %get-tuple-element.4.first, f32[32,4096]{1,0:T(8,128)} %get-tuple-element.5.second), custom_call_target="tpu_custom_call" | custom-call | tf_op jit(solution)/shard_map/pallas_call | solution.py:454
where the time goes:
time: 53.2 us; the launch traced here: 53 us
  Pallas kernels  52.2 us (98%)
  between operations  0.8 us (2%)
    pallas_call x1, Pallas kernels, body(): pl.pallas_call(kernel, out_shape=(out, out), in_specs=[pl.BlockSpec(memor...  50.2 us
    pallas_call x1, Pallas kernels, body(): pl.pallas_call(copy_out, out_shape=(out, out), in_specs=[hbm, hbm], out_s...  1.98 us

commit v1 on v0

--- a/solution.py
+++ b/solution.py
@@ -348,9 +348,9 @@
     for part in range(2):
         apply(1, 1, vals.at[1, 1], part, True)
     vals_mate.wait_recv()
-    for part in range(2):
-        apply(2, near_slot, halo_vals.at[1, 0], part)
+    apply(2, near_slot, halo_vals.at[1, 0], 0)
     second.after_z()
+    apply(2, near_slot, halo_vals.at[1, 0], 1)
     vals_far.wait_recv()
     edges(vals.at[1], halo_vals.at[1])
     for part in range(2):
@@ -360,11 +360,10 @@
         acc[l] += far(l, 0)
     second.after_xy()
     second.finish_high()
+    more = [pltpu.make_async_copy(acc.at[l], out2.at[:, pl.ds(l * LEAF, LEAF)], out_sem.at[2 + l]) for l in range(2)]
     for l in range(2):
         acc[l] += far(l, 1)
-    more = [pltpu.make_async_copy(acc.at[l], out2.at[:, pl.ds(l * LEAF, LEAF)], out_sem.at[2 + l]) for l in range(2)]
-    for copy in more:
-        copy.start()
+        more[l].start()
     for copy in sent:
         copy.wait_send()
     for copy in outs + more:

time: 53.2 us -> 53.1 us (level)
  no operation moved by 1% of the time
where the time goes in v1:
time: 53.1 us; the launch traced here: 52.9 us
  Pallas kernels  52.1 us (98%)
  between operations  0.8 us (2%)
    pallas_call x1, Pallas kernels, body(): pl.pallas_call(kernel, out_shape=(out, out), in_specs=[pl.BlockSpec(memor...  50.1 us
    pallas_call x1, Pallas kernels, body(): pl.pallas_call(copy_out, out_shape=(out, out), in_specs=[hbm, hbm], out_s...  1.98 us

profile of v1, /device:TPU:1, one launch (start us, length us, event | category | flops | bytes accessed | tf_op | source)
XLA Modules:
  0.0 52.9 jit_solution(13656257134866971053)
XLA Ops:
  0.6 50.1 %shard_map.77 = (f32[32,4096]{1,0:T(8,128)}, f32[32,4096]{1,0:T(8,128)}) custom-call(s32[2]{0:T(128)} %near.1, s32[1,4096]{1,0:T(1,128)} %bitcast.5, bf16[32,4096]{1,0:T(8,128)(2,1)} %rs_hbm.1, bf16[64,4096]{1,0:T(8,128)(2,1)} %pts_hbm.1, bf16[512,4096]{1,0:T(8,128)(2,1)} %bitcast.3, bf16[512,4096]{1,0:T(8,128)(2,1)} %bitcast.4), custom_call_target="tpu_custom_call" | custom-call | tf_op jit(solution)/shard_map/pallas_call | solution.py:399
  50.8 2.0 %shard_map.78 = (f32[32,4096]{1,0:T(8,128)}, f32[32,4096]{1,0:T(8,128)}) custom-call(f32[32,4096]{1,0:T(8,128)} %get-tuple-element.4.first, f32[32,4096]{1,0:T(8,128)} %get-tuple-element.5.second), custom_call_target="tpu_custom_call" | custom-call | tf_op jit(solution)/shard_map/pallas_call | solution.py:453
